TPU v7x, 256 devices: a whole 4x4x8 slice. The times are simulated.
256 devices in a mesh: section: 8 (over x, core), expert: 32 (over y, z).
Axes of the slice: x: 4, y: 4, z: 8, core: 2. Of those that a mesh axis runs over, the one named last changes fastest.
Arguments:
- layer_inputs: bfloat16 [8, 4, 1024, 2048], P('section', None, 'expert'), may hold values from -6 to 6
- expert_ids: int32 [8, 4, 1024, 3], P('section', None, 'expert'), may hold values from 0 to 31, all different within a row; in each aligned block of 32 rows (0 to 31, 32 to 63, ..., all dimensions but the last counted through in order) at most 4 rows name the same one
- gate_weights: float32 [8, 4, 1024, 3], P('section', None, 'expert'), may hold values from 0.1 to 0.6
- norm_gain: float32 [8, 2048], P('section'), may hold values from 0.1 to 1.9
- w_gate: bfloat16 [8, 32, 2048, 256], P('section', 'expert'), may hold values from -0.125 to 0.125
- w_up: bfloat16 [8, 32, 2048, 256], P('section', 'expert'), may hold values from -0.125 to 0.125
- w_down: bfloat16 [8, 32, 256, 2048], P('section', 'expert'), may hold values from -0.375 to 0.375
- top_cotangent: bfloat16 [4, 1024, 2048], P(None, 'expert'), may hold values from -6 to 6
Outputs:
- input_grads: bfloat16 [8, 4, 1024, 2048], P('section', None, 'expert')
- grad_gate: bfloat16 [8, 32, 2048, 256], P('section', 'expert')
- grad_up: bfloat16 [8, 32, 2048, 256], P('section', 'expert')
- grad_down: bfloat16 [8, 32, 256, 2048], P('section', 'expert')
- gain_grads: float32 [8, 2048], P('section')
Inputs may be any that keep to these rules, and one draw needn't show every extreme that they name: `expert_ids`: each token names 3 different experts. Within the 32 tokens of one layer, one micro-batch and one index of expert, no expert is named by more than 4 tokens, a bound that some block reaches.
All inputs are finite; a program needn't handle non-finite values.
Results may differ from a plain program's by a relative error of at most 0.03.
Values may be sent and summed in bfloat16 or wider, within the bound.
A program may use at most 64 MiB of HBM per device.

v0:
```python
import jax
import jax.numpy as jnp
from jax import lax
from jax.sharding import PartitionSpec as P

epsilon = 1e-06


def shifted(value, axis, steps):
    count = lax.axis_size(axis)
    initial, last = (max(0, -steps), min(count, count - steps))
    return lax.ppermute(value, axis, [(source, source + steps) for source in range(initial, last)])


def normalize(inputs, gain):
    values = inputs.astype(jnp.float32)
    scales = lax.rsqrt(jnp.mean(values * values, axis=-1, keepdims=True) + epsilon)
    unit_rows = values * scales
    return (unit_rows, scales, (unit_rows * gain).astype(jnp.bfloat16))


def placement_matrix(routed, experts, capacity):
    flat_ids = routed.reshape(-1)
    one_hot = (flat_ids[:, None] == jnp.arange(experts, dtype=jnp.int32)[None, :]).astype(jnp.int32)
    earlier = jnp.cumsum(one_hot, axis=0) - one_hot
    slot_index = jnp.sum(earlier * one_hot, axis=1)
    target = flat_ids * capacity + slot_index
    return (jnp.arange(experts * capacity, dtype=jnp.int32)[:, None] == target[None, :]).astype(
        jnp.bfloat16
    )


def spread_rows(placing, row_block, experts, capacity):
    width = row_block.shape[-1]
    spread = jnp.dot(placing, row_block, preferred_element_type=jnp.float32).astype(jnp.bfloat16)
    return spread.reshape(experts, capacity, width)


def contract(left, right, left_dim, right_dim):
    return lax.dot_general(
        left, right, (((left_dim,), (right_dim,)), ((), ())), preferred_element_type=jnp.float32
    )


def expert_backward(input_rows, scaled_rows, gate_mat, up_mat, down_mat):
    pre_gate = jnp.dot(input_rows, gate_mat, preferred_element_type=jnp.float32)
    pre_up = jnp.dot(input_rows, up_mat, preferred_element_type=jnp.float32)
    sigma = jax.nn.sigmoid(pre_gate)
    silu_gate = pre_gate * sigma
    activated = (silu_gate * pre_up).astype(jnp.bfloat16)
    d_act = contract(scaled_rows, down_mat, 1, 1)
    d_gate = (d_act * pre_up * sigma * (1.0 + pre_gate * (1.0 - sigma))).astype(jnp.bfloat16)
    d_up = (d_act * silu_gate).astype(jnp.bfloat16)
    returned = (contract(d_gate, gate_mat, 1, 1) + contract(d_up, up_mat, 1, 1)).astype(
        jnp.bfloat16
    )
    return (
        returned,
        contract(input_rows, d_gate, 0, 0),
        contract(input_rows, d_up, 0, 0),
        contract(activated, scaled_rows, 0, 0),
    )


def local(layer_inputs, expert_ids, gate_weights, norm_gain, w_gate, w_up, w_down, top_cotangent):
    sections = lax.axis_size("section")
    experts = lax.axis_size("expert")
    section_index = lax.axis_index("section")
    micro_count = layer_inputs.shape[1]
    tok_rows = layer_inputs.shape[2]
    width = layer_inputs.shape[3]
    top_count = expert_ids.shape[3]
    capacity = max(2, 3 * tok_rows * top_count // (2 * experts))
    gain = norm_gain[0]
    gate_mat = w_gate[0, 0]
    up_mat = w_up[0, 0]
    down_mat = w_down[0, 0]
    hidden = gate_mat.shape[1]

    def one_round(round_index, carry):
        incoming, acc_gate, acc_up, acc_down, acc_gain, results = carry
        micro = round_index - (sections - 1 - section_index)
        active = (micro >= 0) & (micro < micro_count)
        picked = jnp.clip(micro, 0, micro_count - 1)
        cotangent = jnp.where(section_index == sections - 1, top_cotangent[picked], incoming)
        unit_rows, scales, normed = normalize(layer_inputs[0, picked], gain)
        placing = placement_matrix(expert_ids[0, picked], experts, capacity)
        scaled = (
            gate_weights[0, picked][:, :, None] * cotangent.astype(jnp.float32)[:, None, :]
        ).astype(jnp.bfloat16)
        scaled = jnp.where(active, scaled, jnp.zeros_like(scaled)).reshape(-1, width)
        sent_cot = spread_rows(placing, scaled, experts, capacity)
        sent_inputs = spread_rows(placing, jnp.repeat(normed, top_count, axis=0), experts, capacity)
        recv_inputs, recv_cot = (
            lax.all_to_all(sent_inputs, "expert", split_axis=0, concat_axis=0, tiled=True),
            lax.all_to_all(sent_cot, "expert", split_axis=0, concat_axis=0, tiled=True),
        )
        returned, inc_gate, inc_up, inc_down = expert_backward(
            recv_inputs.reshape(-1, width), recv_cot.reshape(-1, width), gate_mat, up_mat, down_mat
        )
        gathered = lax.all_to_all(
            returned.reshape(experts, capacity, width),
            "expert",
            split_axis=0,
            concat_axis=0,
            tiled=True,
        )
        row_grads = jnp.dot(
            placing.T, gathered.reshape(-1, width), preferred_element_type=jnp.float32
        )
        d_normed = jnp.sum(row_grads.reshape(tok_rows, top_count, width), axis=1)
        gain_term = jnp.where(
            active, jnp.sum(d_normed * unit_rows, axis=0), jnp.zeros((width,), jnp.float32)
        )
        scaled_grad = d_normed * gain
        input_grad = cotangent.astype(jnp.float32) + scales * (
            scaled_grad - unit_rows * jnp.mean(scaled_grad * unit_rows, axis=-1, keepdims=True)
        )
        input_grad = input_grad.astype(jnp.bfloat16)
        results = results.at[picked].set(jnp.where(active, input_grad, results[picked]))
        passed = shifted(input_grad, "section", -1)
        return (
            passed,
            acc_gate + inc_gate,
            acc_up + inc_up,
            acc_down + inc_down,
            acc_gain + gain_term,
            results,
        )

    initial = (
        jnp.zeros((tok_rows, width), jnp.bfloat16),
        jnp.zeros((width, hidden), jnp.float32),
        jnp.zeros((width, hidden), jnp.float32),
        jnp.zeros((hidden, width), jnp.float32),
        jnp.zeros((width,), jnp.float32),
        jnp.zeros((micro_count, tok_rows, width), jnp.bfloat16),
    )
    final = lax.fori_loop(0, sections + micro_count - 1, one_round, initial)
    gain_total = lax.psum(final[4], "expert")
    return (
        final[5][None],
        final[1].astype(jnp.bfloat16)[None, None],
        final[2].astype(jnp.bfloat16)[None, None],
        final[3].astype(jnp.bfloat16)[None, None],
        gain_total[None],
    )


def solution(mesh):
    in_specs = (
        P("section", None, "expert", None),
        P("section", None, "expert", None),
        P("section", None, "expert", None),
        P("section", None),
        P("section", "expert", None, None),
        P("section", "expert", None, None),
        P("section", "expert", None, None),
        P(None, "expert", None),
    )
    out_specs = (
        P("section", None, "expert", None),
        P("section", "expert", None, None),
        P("section", "expert", None, None),
        P("section", "expert", None, None),
        P("section", None),
    )
    return jax.shard_map(local, mesh=mesh, in_specs=in_specs, out_specs=out_specs, check_vma=False)
```

profile of v0, /device:TPU:4, one launch (start us, length us, event | category | flops | bytes accessed | tf_op | source)
XLA Modules:
  0.0 1061.4 jit_solution(14094746738491032428)
XLA Ops:
  1.5 980.2 %while.27 = (s32[]{:T(128)}, bf16[32,2048]{1,0:T(8,128)(2,1)S(1)}, f32[2048,256]{1,0:T(8,128)}, f32[2048,256]{1,0:T(8,128)}, f32[256,2048]{1,0:T(8,128)}, /*inde...) while((s32[]{:T(128)}, bf16[32,2048]{1,0:T(8,128)(2,1)S(1)}, ...), condition=%wide.region_8.9_spmd.clone, body=%wide.region_0.8_spmd.clone.sunk | while | flops 1232332928 | bytes 92017160 | solution.py:139
  6.8 11.5 %all-to-all-start = ((bf16[32,4,2048]{2,1,0:T(4,128)(2,1)}), bf16[32,4,2048]{2,1,0:T(4,128)(2,1)S(1)}, u32[]{:S(2)}, u32[]{:S(2)}) async-start(bf16[32,4,2048]{2,1,0:T(4,128)(2,1)} %reshape.241), calls=%async_computation | async-start | bytes 1048576 | tf_op jit(solution)/shard_map/while/body/eval_jaxpr/all_to_all | solution.py:95
  22.2 12.9 %all-to-all-done = bf16[32,4,2048]{2,1,0:T(4,128)(2,1)S(1)} async-done(((bf16[32,4,2048]{2,1,0:T(4,128)(2,1)}), bf16[32,4,2048]{2,1,0:T(4,128)(2,1)S(1)}, u32[]{:S(2)}, u32[]{:S(2)}) %all-to-all-start) | async-done | bytes 524320 | tf_op jit(solution)/shard_map/while/body/eval_jaxpr/all_to_all | solution.py:95
  35.2 5.7 all-to-all-start.1
  44.8 12.6 %all-to-all-done.1 = bf16[32,4,2048]{2,1,0:T(4,128)(2,1)} async-done(((bf16[32,4,2048]{2,1,0:T(4,128)(2,1)}), bf16[32,4,2048]{2,1,0:T(4,128)(2,1)}, u32[]{:S(2)}, u32[]{:S(2)}) %all-to-all-start.1) | async-done | bytes 524320 | tf_op jit(solution)/shard_map/while/body/eval_jaxpr/all_to_all | solution.py:96
  64.4 5.4 all-to-all-start.2
  76.1 10.2 all-to-all-done.2
  108.2 13.8 %all-to-all-done = bf16[32,4,2048]{2,1,0:T(4,128)(2,1)S(1)} async-done(((bf16[32,4,2048]{2,1,0:T(4,128)(2,1)}), bf16[32,4,2048]{2,1,0:T(4,128)(2,1)S(1)}, u32[]{:S(2)}, u32[]{:S(2)}) %all-to-all-start) | async-done | bytes 524320 | tf_op jit(solution)/shard_map/while/body/eval_jaxpr/all_to_all | solution.py:95
  122.0 6.3 all-to-all-start.1
  132.1 13.1 %all-to-all-done.1 = bf16[32,4,2048]{2,1,0:T(4,128)(2,1)} async-done(((bf16[32,4,2048]{2,1,0:T(4,128)(2,1)}), bf16[32,4,2048]{2,1,0:T(4,128)(2,1)}, u32[]{:S(2)}, u32[]{:S(2)}) %all-to-all-start.1) | async-done | bytes 524320 | tf_op jit(solution)/shard_map/while/body/eval_jaxpr/all_to_all | solution.py:96
  152.2 5.9 all-to-all-start.2
  166.0 9.0 all-to-all-done.2
  187.8 5.4 all-to-all-start
  197.1 13.8 %all-to-all-done = bf16[32,4,2048]{2,1,0:T(4,128)(2,1)S(1)} async-done(((bf16[32,4,2048]{2,1,0:T(4,128)(2,1)}), bf16[32,4,2048]{2,1,0:T(4,128)(2,1)S(1)}, u32[]{:S(2)}, u32[]{:S(2)}) %all-to-all-start) | async-done | bytes 524320 | tf_op jit(solution)/shard_map/while/body/eval_jaxpr/all_to_all | solution.py:95
  211.0 6.1 all-to-all-start.1
  220.9 13.0 %all-to-all-done.1 = bf16[32,4,2048]{2,1,0:T(4,128)(2,1)} async-done(((bf16[32,4,2048]{2,1,0:T(4,128)(2,1)}), bf16[32,4,2048]{2,1,0:T(4,128)(2,1)}, u32[]{:S(2)}, u32[]{:S(2)}) %all-to-all-start.1) | async-done | bytes 524320 | tf_op jit(solution)/shard_map/while/body/eval_jaxpr/all_to_all | solution.py:96
  240.9 5.9 all-to-all-start.2
  254.7 9.0 all-to-all-done.2
  285.8 14.2 %all-to-all-done = bf16[32,4,2048]{2,1,0:T(4,128)(2,1)S(1)} async-done(((bf16[32,4,2048]{2,1,0:T(4,128)(2,1)}), bf16[32,4,2048]{2,1,0:T(4,128)(2,1)S(1)}, u32[]{:S(2)}, u32[]{:S(2)}) %all-to-all-start) | async-done | bytes 524320 | tf_op jit(solution)/shard_map/while/body/eval_jaxpr/all_to_all | solution.py:95
  300.0 5.9 all-to-all-start.1
  309.7 13.1 %all-to-all-done.1 = bf16[32,4,2048]{2,1,0:T(4,128)(2,1)} async-done(((bf16[32,4,2048]{2,1,0:T(4,128)(2,1)}), bf16[32,4,2048]{2,1,0:T(4,128)(2,1)}, u32[]{:S(2)}, u32[]{:S(2)}) %all-to-all-start.1) | async-done | bytes 524320 | tf_op jit(solution)/shard_map/while/body/eval_jaxpr/all_to_all | solution.py:96
  329.8 5.9 all-to-all-start.2
  343.6 9.0 all-to-all-done.2
  365.4 5.4 all-to-all-start
  374.7 13.8 %all-to-all-done = bf16[32,4,2048]{2,1,0:T(4,128)(2,1)S(1)} async-done(((bf16[32,4,2048]{2,1,0:T(4,128)(2,1)}), bf16[32,4,2048]{2,1,0:T(4,128)(2,1)S(1)}, u32[]{:S(2)}, u32[]{:S(2)}) %all-to-all-start) | async-done | bytes 524320 | tf_op jit(solution)/shard_map/while/body/eval_jaxpr/all_to_all | solution.py:95
  388.6 6.1 all-to-all-start.1
  398.5 13.0 %all-to-all-done.1 = bf16[32,4,2048]{2,1,0:T(4,128)(2,1)} async-done(((bf16[32,4,2048]{2,1,0:T(4,128)(2,1)}), bf16[32,4,2048]{2,1,0:T(4,128)(2,1)}, u32[]{:S(2)}, u32[]{:S(2)}) %all-to-all-start.1) | async-done | bytes 524320 | tf_op jit(solution)/shard_map/while/body/eval_jaxpr/all_to_all | solution.py:96
  418.5 5.9 all-to-all-start.2
  432.3 9.0 all-to-all-done.2
  454.2 5.3 all-to-all-start
  463.4 14.2 %all-to-all-done = bf16[32,4,2048]{2,1,0:T(4,128)(2,1)S(1)} async-done(((bf16[32,4,2048]{2,1,0:T(4,128)(2,1)}), bf16[32,4,2048]{2,1,0:T(4,128)(2,1)S(1)}, u32[]{:S(2)}, u32[]{:S(2)}) %all-to-all-start) | async-done | bytes 524320 | tf_op jit(solution)/shard_map/while/body/eval_jaxpr/all_to_all | solution.py:95
  477.6 5.9 all-to-all-start.1
  487.4 13.1 %all-to-all-done.1 = bf16[32,4,2048]{2,1,0:T(4,128)(2,1)} async-done(((bf16[32,4,2048]{2,1,0:T(4,128)(2,1)}), bf16[32,4,2048]{2,1,0:T(4,128)(2,1)}, u32[]{:S(2)}, u32[]{:S(2)}) %all-to-all-start.1) | async-done | bytes 524320 | tf_op jit(solution)/shard_map/while/body/eval_jaxpr/all_to_all | solution.py:96
  507.4 5.9 all-to-all-start.2
  521.2 9.0 all-to-all-done.2
  543.0 5.4 all-to-all-start
  552.3 13.8 %all-to-all-done = bf16[32,4,2048]{2,1,0:T(4,128)(2,1)S(1)} async-done(((bf16[32,4,2048]{2,1,0:T(4,128)(2,1)}), bf16[32,4,2048]{2,1,0:T(4,128)(2,1)S(1)}, u32[]{:S(2)}, u32[]{:S(2)}) %all-to-all-start) | async-done | bytes 524320 | tf_op jit(solution)/shard_map/while/body/eval_jaxpr/all_to_all | solution.py:95
  566.2 6.1 all-to-all-start.1
  576.1 13.0 %all-to-all-done.1 = bf16[32,4,2048]{2,1,0:T(4,128)(2,1)} async-done(((bf16[32,4,2048]{2,1,0:T(4,128)(2,1)}), bf16[32,4,2048]{2,1,0:T(4,128)(2,1)}, u32[]{:S(2)}, u32[]{:S(2)}) %all-to-all-start.1) | async-done | bytes 524320 | tf_op jit(solution)/shard_map/while/body/eval_jaxpr/all_to_all | solution.py:96
  596.1 5.9 all-to-all-start.2
  610.0 9.0 all-to-all-done.2
  641.0 14.2 %all-to-all-done = bf16[32,4,2048]{2,1,0:T(4,128)(2,1)S(1)} async-done(((bf16[32,4,2048]{2,1,0:T(4,128)(2,1)}), bf16[32,4,2048]{2,1,0:T(4,128)(2,1)S(1)}, u32[]{:S(2)}, u32[]{:S(2)}) %all-to-all-start) | async-done | bytes 524320 | tf_op jit(solution)/shard_map/while/body/eval_jaxpr/all_to_all | solution.py:95
  655.2 5.9 all-to-all-start.1
  665.0 13.1 %all-to-all-done.1 = bf16[32,4,2048]{2,1,0:T(4,128)(2,1)} async-done(((bf16[32,4,2048]{2,1,0:T(4,128)(2,1)}), bf16[32,4,2048]{2,1,0:T(4,128)(2,1)}, u32[]{:S(2)}, u32[]{:S(2)}) %all-to-all-start.1) | async-done | bytes 524320 | tf_op jit(solution)/shard_map/while/body/eval_jaxpr/all_to_all | solution.py:96
  685.0 5.9 all-to-all-start.2
  698.9 9.0 all-to-all-done.2
  720.7 5.4 all-to-all-start
  730.0 13.8 %all-to-all-done = bf16[32,4,2048]{2,1,0:T(4,128)(2,1)S(1)} async-done(((bf16[32,4,2048]{2,1,0:T(4,128)(2,1)}), bf16[32,4,2048]{2,1,0:T(4,128)(2,1)S(1)}, u32[]{:S(2)}, u32[]{:S(2)}) %all-to-all-start) | async-done | bytes 524320 | tf_op jit(solution)/shard_map/while/body/eval_jaxpr/all_to_all | solution.py:95
  743.8 6.1 all-to-all-start.1
  753.8 13.0 %all-to-all-done.1 = bf16[32,4,2048]{2,1,0:T(4,128)(2,1)} async-done(((bf16[32,4,2048]{2,1,0:T(4,128)(2,1)}), bf16[32,4,2048]{2,1,0:T(4,128)(2,1)}, u32[]{:S(2)}, u32[]{:S(2)}) %all-to-all-start.1) | async-done | bytes 524320 | tf_op jit(solution)/shard_map/while/body/eval_jaxpr/all_to_all | solution.py:96
  773.7 5.9 all-to-all-start.2
  787.6 9.0 all-to-all-done.2
  818.6 14.2 %all-to-all-done = bf16[32,4,2048]{2,1,0:T(4,128)(2,1)S(1)} async-done(((bf16[32,4,2048]{2,1,0:T(4,128)(2,1)}), bf16[32,4,2048]{2,1,0:T(4,128)(2,1)S(1)}, u32[]{:S(2)}, u32[]{:S(2)}) %all-to-all-start) | async-done | bytes 524320 | tf_op jit(solution)/shard_map/while/body/eval_jaxpr/all_to_all | solution.py:95
  832.8 5.9 all-to-all-start.1
  842.6 13.1 %all-to-all-done.1 = bf16[32,4,2048]{2,1,0:T(4,128)(2,1)} async-done(((bf16[32,4,2048]{2,1,0:T(4,128)(2,1)}), bf16[32,4,2048]{2,1,0:T(4,128)(2,1)}, u32[]{:S(2)}, u32[]{:S(2)}) %all-to-all-start.1) | async-done | bytes 524320 | tf_op jit(solution)/shard_map/while/body/eval_jaxpr/all_to_all | solution.py:96
  862.6 5.9 all-to-all-start.2
  876.5 9.0 all-to-all-done.2
  898.3 5.4 all-to-all-start
  907.6 13.8 %all-to-all-done = bf16[32,4,2048]{2,1,0:T(4,128)(2,1)S(1)} async-done(((bf16[32,4,2048]{2,1,0:T(4,128)(2,1)}), bf16[32,4,2048]{2,1,0:T(4,128)(2,1)S(1)}, u32[]{:S(2)}, u32[]{:S(2)}) %all-to-all-start) | async-done | bytes 524320 | tf_op jit(solution)/shard_map/while/body/eval_jaxpr/all_to_all | solution.py:95
  921.4 6.1 all-to-all-start.1
  931.4 13.0 %all-to-all-done.1 = bf16[32,4,2048]{2,1,0:T(4,128)(2,1)} async-done(((bf16[32,4,2048]{2,1,0:T(4,128)(2,1)}), bf16[32,4,2048]{2,1,0:T(4,128)(2,1)}, u32[]{:S(2)}, u32[]{:S(2)}) %all-to-all-start.1) | async-done | bytes 524320 | tf_op jit(solution)/shard_map/while/body/eval_jaxpr/all_to_all | solution.py:96
  951.3 5.9 all-to-all-start.2
  965.2 9.0 all-to-all-done.2
  981.8 73.8 %psum.7 = f32[1,2048]{1,0:T(1,128)} all-reduce(f32[1,2048]{1,0:T(1,128)} %bitcast.110), channel_id=1, replica_groups=mesh['section'=8,'expert'=32] {'expert'}, use_global_device_ids=true, to_apply=%region_9.10 | all-reduce | flops 2048 | bytes 16384 | tf_op jit(solution)/shard_map/psum | solution.py:140
  (905 shorter events, 412.9 us)
Async XLA Ops:
  6.8 28.4 %all-to-all-start = ((bf16[32,4,2048]{2,1,0:T(4,128)(2,1)}), bf16[32,4,2048]{2,1,0:T(4,128)(2,1)S(1)}, u32[]{:S(2)}, u32[]{:S(2)}) async-start(bf16[32,4,2048]{2,1,0:T(4,128)(2,1)} %reshape.241), calls=%async_computation | async-start | bytes 1048576 | tf_op jit(solution)/shard_map/while/body/eval_jaxpr/all_to_all | solution.py:95
  35.2 22.3 %all-to-all-start.1 = ((bf16[32,4,2048]{2,1,0:T(4,128)(2,1)}), bf16[32,4,2048]{2,1,0:T(4,128)(2,1)}, u32[]{:S(2)}, u32[]{:S(2)}) async-start(bf16[32,4,2048]{2,1,0:T(4,128)(2,1)} %reshape.243), calls=%async_computation.1 | async-start | bytes 1048576 | tf_op jit(solution)/shard_map/while/body/eval_jaxpr/all_to_all | solution.py:96
  64.4 21.9 %all-to-all-start.2 = ((bf16[32,4,2048]{2,1,0:T(4,128)(2,1)}), bf16[32,4,2048]{2,1,0:T(4,128)(2,1)}, u32[]{:S(2)}, u32[]{:S(2)}) async-start(bf16[32,4,2048]{2,1,0:T(4,128)(2,1)} %reshape.245), calls=%async_computation.2 | async-start | bytes 1048576 | tf_op jit(solution)/shard_map/while/body/eval_jaxpr/all_to_all | solution.py:101
  89.5 4.4 collective-permute-start
  99.2 22.8 %all-to-all-start = ((bf16[32,4,2048]{2,1,0:T(4,128)(2,1)}), bf16[32,4,2048]{2,1,0:T(4,128)(2,1)S(1)}, u32[]{:S(2)}, u32[]{:S(2)}) async-start(bf16[32,4,2048]{2,1,0:T(4,128)(2,1)} %reshape.241), calls=%async_computation | async-start | bytes 1048576 | tf_op jit(solution)/shard_map/while/body/eval_jaxpr/all_to_all | solution.py:95
  106.8 24.0 %copy-start.1 = (bf16[2048,256]{1,0:T(8,128)(2,1)S(1)}, bf16[2048,256]{1,0:T(8,128)(2,1)}, u32[]{:S(2)}) copy-start(bf16[2048,256]{1,0:T(8,128)(2,1)} %get-tuple-element.706) | copy-start | bytes 3145732 | tf_op jit(solution)/shard_map/while
  108.2 22.9 %copy-start = (bf16[2048,256]{1,0:T(8,128)(2,1)S(1)}, bf16[2048,256]{1,0:T(8,128)(2,1)}, u32[]{:S(2)}) copy-start(bf16[2048,256]{1,0:T(8,128)(2,1)} %get-tuple-element.707) | copy-start | bytes 3145732 | tf_op jit(solution)/shard_map/while
  122.0 23.2 %all-to-all-start.1 = ((bf16[32,4,2048]{2,1,0:T(4,128)(2,1)}), bf16[32,4,2048]{2,1,0:T(4,128)(2,1)}, u32[]{:S(2)}, u32[]{:S(2)}) async-start(bf16[32,4,2048]{2,1,0:T(4,128)(2,1)} %reshape.243), calls=%async_computation.1 | async-start | bytes 1048576 | tf_op jit(solution)/shard_map/while/body/eval_jaxpr/all_to_all | solution.py:96
  152.2 22.8 %all-to-all-start.2 = ((bf16[32,4,2048]{2,1,0:T(4,128)(2,1)}), bf16[32,4,2048]{2,1,0:T(4,128)(2,1)}, u32[]{:S(2)}, u32[]{:S(2)}) async-start(bf16[32,4,2048]{2,1,0:T(4,128)(2,1)} %reshape.245), calls=%async_computation.2 | async-start | bytes 1048576 | tf_op jit(solution)/shard_map/while/body/eval_jaxpr/all_to_all | solution.py:101
  178.1 4.4 collective-permute-start
  187.8 23.1 %all-to-all-start = ((bf16[32,4,2048]{2,1,0:T(4,128)(2,1)}), bf16[32,4,2048]{2,1,0:T(4,128)(2,1)S(1)}, u32[]{:S(2)}, u32[]{:S(2)}) async-start(bf16[32,4,2048]{2,1,0:T(4,128)(2,1)} %reshape.241), calls=%async_computation | async-start | bytes 1048576 | tf_op jit(solution)/shard_map/while/body/eval_jaxpr/all_to_all | solution.py:95
  195.7 23.9 %copy-start.1 = (bf16[2048,256]{1,0:T(8,128)(2,1)S(1)}, bf16[2048,256]{1,0:T(8,128)(2,1)}, u32[]{:S(2)}) copy-start(bf16[2048,256]{1,0:T(8,128)(2,1)} %get-tuple-element.706) | copy-start | bytes 3145732 | tf_op jit(solution)/shard_map/while
  197.1 22.8 %copy-start = (bf16[2048,256]{1,0:T(8,128)(2,1)S(1)}, bf16[2048,256]{1,0:T(8,128)(2,1)}, u32[]{:S(2)}) copy-start(bf16[2048,256]{1,0:T(8,128)(2,1)} %get-tuple-element.707) | copy-start | bytes 3145732 | tf_op jit(solution)/shard_map/while
  211.0 22.9 %all-to-all-start.1 = ((bf16[32,4,2048]{2,1,0:T(4,128)(2,1)}), bf16[32,4,2048]{2,1,0:T(4,128)(2,1)}, u32[]{:S(2)}, u32[]{:S(2)}) async-start(bf16[32,4,2048]{2,1,0:T(4,128)(2,1)} %reshape.243), calls=%async_computation.1 | async-start | bytes 1048576 | tf_op jit(solution)/shard_map/while/body/eval_jaxpr/all_to_all | solution.py:96
  240.9 22.9 %all-to-all-start.2 = ((bf16[32,4,2048]{2,1,0:T(4,128)(2,1)}), bf16[32,4,2048]{2,1,0:T(4,128)(2,1)}, u32[]{:S(2)}, u32[]{:S(2)}) async-start(bf16[32,4,2048]{2,1,0:T(4,128)(2,1)} %reshape.245), calls=%async_computation.2 | async-start | bytes 1048576 | tf_op jit(solution)/shard_map/while/body/eval_jaxpr/all_to_all | solution.py:101
  266.9 4.4 collective-permute-start
  276.6 23.4 %all-to-all-start = ((bf16[32,4,2048]{2,1,0:T(4,128)(2,1)}), bf16[32,4,2048]{2,1,0:T(4,128)(2,1)S(1)}, u32[]{:S(2)}, u32[]{:S(2)}) async-start(bf16[32,4,2048]{2,1,0:T(4,128)(2,1)} %reshape.241), calls=%async_computation | async-start | bytes 1048576 | tf_op jit(solution)/shard_map/while/body/eval_jaxpr/all_to_all | solution.py:95
  284.4 24.0 %copy-start.1 = (bf16[2048,256]{1,0:T(8,128)(2,1)S(1)}, bf16[2048,256]{1,0:T(8,128)(2,1)}, u32[]{:S(2)}) copy-start(bf16[2048,256]{1,0:T(8,128)(2,1)} %get-tuple-element.706) | copy-start | bytes 3145732 | tf_op jit(solution)/shard_map/while
  285.8 23.0 %copy-start = (bf16[2048,256]{1,0:T(8,128)(2,1)S(1)}, bf16[2048,256]{1,0:T(8,128)(2,1)}, u32[]{:S(2)}) copy-start(bf16[2048,256]{1,0:T(8,128)(2,1)} %get-tuple-element.707) | copy-start | bytes 3145732 | tf_op jit(solution)/shard_map/while
  300.0 22.9 %all-to-all-start.1 = ((bf16[32,4,2048]{2,1,0:T(4,128)(2,1)}), bf16[32,4,2048]{2,1,0:T(4,128)(2,1)}, u32[]{:S(2)}, u32[]{:S(2)}) async-start(bf16[32,4,2048]{2,1,0:T(4,128)(2,1)} %reshape.243), calls=%async_computation.1 | async-start | bytes 1048576 | tf_op jit(solution)/shard_map/while/body/eval_jaxpr/all_to_all | solution.py:96
  329.8 22.8 %all-to-all-start.2 = ((bf16[32,4,2048]{2,1,0:T(4,128)(2,1)}), bf16[32,4,2048]{2,1,0:T(4,128)(2,1)}, u32[]{:S(2)}, u32[]{:S(2)}) async-start(bf16[32,4,2048]{2,1,0:T(4,128)(2,1)} %reshape.245), calls=%async_computation.2 | async-start | bytes 1048576 | tf_op jit(solution)/shard_map/while/body/eval_jaxpr/all_to_all | solution.py:101
  355.7 4.4 collective-permute-start
  365.4 23.1 %all-to-all-start = ((bf16[32,4,2048]{2,1,0:T(4,128)(2,1)}), bf16[32,4,2048]{2,1,0:T(4,128)(2,1)S(1)}, u32[]{:S(2)}, u32[]{:S(2)}) async-start(bf16[32,4,2048]{2,1,0:T(4,128)(2,1)} %reshape.241), calls=%async_computation | async-start | bytes 1048576 | tf_op jit(solution)/shard_map/while/body/eval_jaxpr/all_to_all | solution.py:95
  373.4 23.9 %copy-start.1 = (bf16[2048,256]{1,0:T(8,128)(2,1)S(1)}, bf16[2048,256]{1,0:T(8,128)(2,1)}, u32[]{:S(2)}) copy-start(bf16[2048,256]{1,0:T(8,128)(2,1)} %get-tuple-element.706) | copy-start | bytes 3145732 | tf_op jit(solution)/shard_map/while
  374.7 22.8 %copy-start = (bf16[2048,256]{1,0:T(8,128)(2,1)S(1)}, bf16[2048,256]{1,0:T(8,128)(2,1)}, u32[]{:S(2)}) copy-start(bf16[2048,256]{1,0:T(8,128)(2,1)} %get-tuple-element.707) | copy-start | bytes 3145732 | tf_op jit(solution)/shard_map/while
  388.6 22.9 %all-to-all-start.1 = ((bf16[32,4,2048]{2,1,0:T(4,128)(2,1)}), bf16[32,4,2048]{2,1,0:T(4,128)(2,1)}, u32[]{:S(2)}, u32[]{:S(2)}) async-start(bf16[32,4,2048]{2,1,0:T(4,128)(2,1)} %reshape.243), calls=%async_computation.1 | async-start | bytes 1048576 | tf_op jit(solution)/shard_map/while/body/eval_jaxpr/all_to_all | solution.py:96
  418.5 22.9 %all-to-all-start.2 = ((bf16[32,4,2048]{2,1,0:T(4,128)(2,1)}), bf16[32,4,2048]{2,1,0:T(4,128)(2,1)}, u32[]{:S(2)}, u32[]{:S(2)}) async-start(bf16[32,4,2048]{2,1,0:T(4,128)(2,1)} %reshape.245), calls=%async_computation.2 | async-start | bytes 1048576 | tf_op jit(solution)/shard_map/while/body/eval_jaxpr/all_to_all | solution.py:101
  444.5 4.4 collective-permute-start
  454.2 23.4 %all-to-all-start = ((bf16[32,4,2048]{2,1,0:T(4,128)(2,1)}), bf16[32,4,2048]{2,1,0:T(4,128)(2,1)S(1)}, u32[]{:S(2)}, u32[]{:S(2)}) async-start(bf16[32,4,2048]{2,1,0:T(4,128)(2,1)} %reshape.241), calls=%async_computation | async-start | bytes 1048576 | tf_op jit(solution)/shard_map/while/body/eval_jaxpr/all_to_all | solution.py:95
  462.0 24.0 %copy-start.1 = (bf16[2048,256]{1,0:T(8,128)(2,1)S(1)}, bf16[2048,256]{1,0:T(8,128)(2,1)}, u32[]{:S(2)}) copy-start(bf16[2048,256]{1,0:T(8,128)(2,1)} %get-tuple-element.706) | copy-start | bytes 3145732 | tf_op jit(solution)/shard_map/while
  463.4 23.0 %copy-start = (bf16[2048,256]{1,0:T(8,128)(2,1)S(1)}, bf16[2048,256]{1,0:T(8,128)(2,1)}, u32[]{:S(2)}) copy-start(bf16[2048,256]{1,0:T(8,128)(2,1)} %get-tuple-element.707) | copy-start | bytes 3145732 | tf_op jit(solution)/shard_map/while
  477.6 22.9 %all-to-all-start.1 = ((bf16[32,4,2048]{2,1,0:T(4,128)(2,1)}), bf16[32,4,2048]{2,1,0:T(4,128)(2,1)}, u32[]{:S(2)}, u32[]{:S(2)}) async-start(bf16[32,4,2048]{2,1,0:T(4,128)(2,1)} %reshape.243), calls=%async_computation.1 | async-start | bytes 1048576 | tf_op jit(solution)/shard_map/while/body/eval_jaxpr/all_to_all | solution.py:96
  507.4 22.8 %all-to-all-start.2 = ((bf16[32,4,2048]{2,1,0:T(4,128)(2,1)}), bf16[32,4,2048]{2,1,0:T(4,128)(2,1)}, u32[]{:S(2)}, u32[]{:S(2)}) async-start(bf16[32,4,2048]{2,1,0:T(4,128)(2,1)} %reshape.245), calls=%async_computation.2 | async-start | bytes 1048576 | tf_op jit(solution)/shard_map/while/body/eval_jaxpr/all_to_all | solution.py:101
  533.4 4.4 collective-permute-start
  543.0 23.1 %all-to-all-start = ((bf16[32,4,2048]{2,1,0:T(4,128)(2,1)}), bf16[32,4,2048]{2,1,0:T(4,128)(2,1)S(1)}, u32[]{:S(2)}, u32[]{:S(2)}) async-start(bf16[32,4,2048]{2,1,0:T(4,128)(2,1)} %reshape.241), calls=%async_computation | async-start | bytes 1048576 | tf_op jit(solution)/shard_map/while/body/eval_jaxpr/all_to_all | solution.py:95
  551.0 23.9 %copy-start.1 = (bf16[2048,256]{1,0:T(8,128)(2,1)S(1)}, bf16[2048,256]{1,0:T(8,128)(2,1)}, u32[]{:S(2)}) copy-start(bf16[2048,256]{1,0:T(8,128)(2,1)} %get-tuple-element.706) | copy-start | bytes 3145732 | tf_op jit(solution)/shard_map/while
  566.2 22.9 %all-to-all-start.1 = ((bf16[32,4,2048]{2,1,0:T(4,128)(2,1)}), bf16[32,4,2048]{2,1,0:T(4,128)(2,1)}, u32[]{:S(2)}, u32[]{:S(2)}) async-start(bf16[32,4,2048]{2,1,0:T(4,128)(2,1)} %reshape.243), calls=%async_computation.1 | async-start | bytes 1048576 | tf_op jit(solution)/shard_map/while/body/eval_jaxpr/all_to_all | solution.py:96
  596.1 22.9 %all-to-all-start.2 = ((bf16[32,4,2048]{2,1,0:T(4,128)(2,1)}), bf16[32,4,2048]{2,1,0:T(4,128)(2,1)}, u32[]{:S(2)}, u32[]{:S(2)}) async-start(bf16[32,4,2048]{2,1,0:T(4,128)(2,1)} %reshape.245), calls=%async_computation.2 | async-start | bytes 1048576 | tf_op jit(solution)/shard_map/while/body/eval_jaxpr/all_to_all | solution.py:101
  622.1 4.4 collective-permute-start
  631.8 23.4 %all-to-all-start = ((bf16[32,4,2048]{2,1,0:T(4,128)(2,1)}), bf16[32,4,2048]{2,1,0:T(4,128)(2,1)S(1)}, u32[]{:S(2)}, u32[]{:S(2)}) async-start(bf16[32,4,2048]{2,1,0:T(4,128)(2,1)} %reshape.241), calls=%async_computation | async-start | bytes 1048576 | tf_op jit(solution)/shard_map/while/body/eval_jaxpr/all_to_all | solution.py:95
  639.6 24.0 %copy-start.1 = (bf16[2048,256]{1,0:T(8,128)(2,1)S(1)}, bf16[2048,256]{1,0:T(8,128)(2,1)}, u32[]{:S(2)}) copy-start(bf16[2048,256]{1,0:T(8,128)(2,1)} %get-tuple-element.706) | copy-start | bytes 3145732 | tf_op jit(solution)/shard_map/while
  641.0 23.0 %copy-start = (bf16[2048,256]{1,0:T(8,128)(2,1)S(1)}, bf16[2048,256]{1,0:T(8,128)(2,1)}, u32[]{:S(2)}) copy-start(bf16[2048,256]{1,0:T(8,128)(2,1)} %get-tuple-element.707) | copy-start | bytes 3145732 | tf_op jit(solution)/shard_map/while
  655.2 22.9 %all-to-all-start.1 = ((bf16[32,4,2048]{2,1,0:T(4,128)(2,1)}), bf16[32,4,2048]{2,1,0:T(4,128)(2,1)}, u32[]{:S(2)}, u32[]{:S(2)}) async-start(bf16[32,4,2048]{2,1,0:T(4,128)(2,1)} %reshape.243), calls=%async_computation.1 | async-start | bytes 1048576 | tf_op jit(solution)/shard_map/while/body/eval_jaxpr/all_to_all | solution.py:96
  685.0 22.8 %all-to-all-start.2 = ((bf16[32,4,2048]{2,1,0:T(4,128)(2,1)}), bf16[32,4,2048]{2,1,0:T(4,128)(2,1)}, u32[]{:S(2)}, u32[]{:S(2)}) async-start(bf16[32,4,2048]{2,1,0:T(4,128)(2,1)} %reshape.245), calls=%async_computation.2 | async-start | bytes 1048576 | tf_op jit(solution)/shard_map/while/body/eval_jaxpr/all_to_all | solution.py:101
  711.0 4.4 collective-permute-start
  720.7 23.1 %all-to-all-start = ((bf16[32,4,2048]{2,1,0:T(4,128)(2,1)}), bf16[32,4,2048]{2,1,0:T(4,128)(2,1)S(1)}, u32[]{:S(2)}, u32[]{:S(2)}) async-start(bf16[32,4,2048]{2,1,0:T(4,128)(2,1)} %reshape.241), calls=%async_computation | async-start | bytes 1048576 | tf_op jit(solution)/shard_map/while/body/eval_jaxpr/all_to_all | solution.py:95
  728.6 23.9 %copy-start.1 = (bf16[2048,256]{1,0:T(8,128)(2,1)S(1)}, bf16[2048,256]{1,0:T(8,128)(2,1)}, u32[]{:S(2)}) copy-start(bf16[2048,256]{1,0:T(8,128)(2,1)} %get-tuple-element.706) | copy-start | bytes 3145732 | tf_op jit(solution)/shard_map/while
  730.0 22.8 %copy-start = (bf16[2048,256]{1,0:T(8,128)(2,1)S(1)}, bf16[2048,256]{1,0:T(8,128)(2,1)}, u32[]{:S(2)}) copy-start(bf16[2048,256]{1,0:T(8,128)(2,1)} %get-tuple-element.707) | copy-start | bytes 3145732 | tf_op jit(solution)/shard_map/while
  743.8 22.9 %all-to-all-start.1 = ((bf16[32,4,2048]{2,1,0:T(4,128)(2,1)}), bf16[32,4,2048]{2,1,0:T(4,128)(2,1)}, u32[]{:S(2)}, u32[]{:S(2)}) async-start(bf16[32,4,2048]{2,1,0:T(4,128)(2,1)} %reshape.243), calls=%async_computation.1 | async-start | bytes 1048576 | tf_op jit(solution)/shard_map/while/body/eval_jaxpr/all_to_all | solution.py:96
  773.7 22.9 %all-to-all-start.2 = ((bf16[32,4,2048]{2,1,0:T(4,128)(2,1)}), bf16[32,4,2048]{2,1,0:T(4,128)(2,1)}, u32[]{:S(2)}, u32[]{:S(2)}) async-start(bf16[32,4,2048]{2,1,0:T(4,128)(2,1)} %reshape.245), calls=%async_computation.2 | async-start | bytes 1048576 | tf_op jit(solution)/shard_map/while/body/eval_jaxpr/all_to_all | solution.py:101
  799.7 4.4 collective-permute-start
  809.4 23.4 %all-to-all-start = ((bf16[32,4,2048]{2,1,0:T(4,128)(2,1)}), bf16[32,4,2048]{2,1,0:T(4,128)(2,1)S(1)}, u32[]{:S(2)}, u32[]{:S(2)}) async-start(bf16[32,4,2048]{2,1,0:T(4,128)(2,1)} %reshape.241), calls=%async_computation | async-start | bytes 1048576 | tf_op jit(solution)/shard_map/while/body/eval_jaxpr/all_to_all | solution.py:95
  817.2 24.0 %copy-start.1 = (bf16[2048,256]{1,0:T(8,128)(2,1)S(1)}, bf16[2048,256]{1,0:T(8,128)(2,1)}, u32[]{:S(2)}) copy-start(bf16[2048,256]{1,0:T(8,128)(2,1)} %get-tuple-element.706) | copy-start | bytes 3145732 | tf_op jit(solution)/shard_map/while
  818.6 23.0 %copy-start = (bf16[2048,256]{1,0:T(8,128)(2,1)S(1)}, bf16[2048,256]{1,0:T(8,128)(2,1)}, u32[]{:S(2)}) copy-start(bf16[2048,256]{1,0:T(8,128)(2,1)} %get-tuple-element.707) | copy-start | bytes 3145732 | tf_op jit(solution)/shard_map/while
  832.8 22.9 %all-to-all-start.1 = ((bf16[32,4,2048]{2,1,0:T(4,128)(2,1)}), bf16[32,4,2048]{2,1,0:T(4,128)(2,1)}, u32[]{:S(2)}, u32[]{:S(2)}) async-start(bf16[32,4,2048]{2,1,0:T(4,128)(2,1)} %reshape.243), calls=%async_computation.1 | async-start | bytes 1048576 | tf_op jit(solution)/shard_map/while/body/eval_jaxpr/all_to_all | solution.py:96
  862.6 22.8 %all-to-all-start.2 = ((bf16[32,4,2048]{2,1,0:T(4,128)(2,1)}), bf16[32,4,2048]{2,1,0:T(4,128)(2,1)}, u32[]{:S(2)}, u32[]{:S(2)}) async-start(bf16[32,4,2048]{2,1,0:T(4,128)(2,1)} %reshape.245), calls=%async_computation.2 | async-start | bytes 1048576 | tf_op jit(solution)/shard_map/while/body/eval_jaxpr/all_to_all | solution.py:101
  888.6 4.4 collective-permute-start
  898.3 23.1 %all-to-all-start = ((bf16[32,4,2048]{2,1,0:T(4,128)(2,1)}), bf16[32,4,2048]{2,1,0:T(4,128)(2,1)S(1)}, u32[]{:S(2)}, u32[]{:S(2)}) async-start(bf16[32,4,2048]{2,1,0:T(4,128)(2,1)} %reshape.241), calls=%async_computation | async-start | bytes 1048576 | tf_op jit(solution)/shard_map/while/body/eval_jaxpr/all_to_all | solution.py:95
  906.2 23.9 %copy-start.1 = (bf16[2048,256]{1,0:T(8,128)(2,1)S(1)}, bf16[2048,256]{1,0:T(8,128)(2,1)}, u32[]{:S(2)}) copy-start(bf16[2048,256]{1,0:T(8,128)(2,1)} %get-tuple-element.706) | copy-start | bytes 3145732 | tf_op jit(solution)/shard_map/while
  907.6 22.8 %copy-start = (bf16[2048,256]{1,0:T(8,128)(2,1)S(1)}, bf16[2048,256]{1,0:T(8,128)(2,1)}, u32[]{:S(2)}) copy-start(bf16[2048,256]{1,0:T(8,128)(2,1)} %get-tuple-element.707) | copy-start | bytes 3145732 | tf_op jit(solution)/shard_map/while
  921.4 22.9 %all-to-all-start.1 = ((bf16[32,4,2048]{2,1,0:T(4,128)(2,1)}), bf16[32,4,2048]{2,1,0:T(4,128)(2,1)}, u32[]{:S(2)}, u32[]{:S(2)}) async-start(bf16[32,4,2048]{2,1,0:T(4,128)(2,1)} %reshape.243), calls=%async_computation.1 | async-start | bytes 1048576 | tf_op jit(solution)/shard_map/while/body/eval_jaxpr/all_to_all | solution.py:96
  951.3 22.9 %all-to-all-start.2 = ((bf16[32,4,2048]{2,1,0:T(4,128)(2,1)}), bf16[32,4,2048]{2,1,0:T(4,128)(2,1)}, u32[]{:S(2)}, u32[]{:S(2)}) async-start(bf16[32,4,2048]{2,1,0:T(4,128)(2,1)} %reshape.245), calls=%async_computation.2 | async-start | bytes 1048576 | tf_op jit(solution)/shard_map/while/body/eval_jaxpr/all_to_all | solution.py:101
  977.4 4.4 collective-permute-start
  981.8 76.5 %copy-start.4 = (f32[2048,256]{1,0:T(8,128)S(1)}, f32[2048,256]{1,0:T(8,128)}, u32[]{:S(2)}) copy-start(f32[2048,256]{1,0:T(8,128)} %get-tuple-element.397) | copy-start | bytes 6291460
  (179 other events, 1276.2 us)
where the time goes:
time: 1070 us; the launch traced here: 1060 us
  waiting for transfers between devices  423 us (40%)
  starting transfers between devices  216 us (20%)
  local copies, waits for them, and re-layouts  147 us (14%)
  matrix products  126 us (12%)
  blocking collectives  73.8 us (7%)
  other arithmetic  71.1 us (7%)
    all_to_all x11, waiting for transfers between devices, one_round(): lax.all_to_all(sent_inputs, 'expert', split_axis=0, concat_axis=0, tiled=...  153 us
    all_to_all x11, waiting for transfers between devices, one_round(): lax.all_to_all(sent_cot, 'expert', split_axis=0, concat_axis=0, tiled=True)  143 us
    dot_general x66, matrix products, contract(): lax.dot_general(left, right, (((left_dim,), (right_dim,)), ((), ())), pre...  102 us
    all_to_all x11, waiting for transfers between devices, one_round(): lax.all_to_all(returned.reshape(experts, capacity, width), 'expert', spli...  100 us
    psum x1, blocking collectives, local(): gain_total = lax.psum(final[4], 'expert')  73.8 us
    all_to_all x11, starting transfers between devices, one_round(): lax.all_to_all(sent_cot, 'expert', split_axis=0, concat_axis=0, tiled=True)  65.9 us
    all_to_all x11, starting transfers between devices, one_round(): lax.all_to_all(returned.reshape(experts, capacity, width), 'expert', spli...  64.5 us
    all_to_all x11, starting transfers between devices, one_round(): lax.all_to_all(sent_inputs, 'expert', split_axis=0, concat_axis=0, tiled=...  64.4 us
  transfers between devices with their start and end apart: 44, of which 44 were waited for; matrix products, arithmetic and copies ran while one was open for 14% of the time, Pallas kernels for 0%

commit v1 on v0

v1 whole, which is shorter than its diff:
```python
import functools

import jax
import jax.numpy as jnp
from jax import lax
from jax.experimental import pallas as pl
from jax.experimental.pallas import tpu as pltpu
from jax.sharding import PartitionSpec as P

epsilon = 1e-06
MESH = pl.DeviceIdType.MESH
F32 = jnp.float32
BF16 = jnp.bfloat16

SECTIONS = 8
NY, NZ = 4, 8
EXPERTS = NY * NZ
MICRO = 4
ROWS = 32
TOP = 3
WIDTH = 2048
HALF = WIDTH // 2
HIDDEN = 256
CAP = 4
BLOCK = 2 * CAP
SLOTS = EXPERTS * BLOCK


def dot(left, right, left_dim=1, right_dim=0):
    return lax.dot_general(
        left, right, (((left_dim,), (right_dim,)), ((), ())), preferred_element_type=F32
    )


def peer(step, index):
    y, z = index // NZ, index % NZ
    across, along = step // NY, step % NY
    dz = NZ // 2 + ((across + 1) // 2) * (1 - 2 * (across % 2))
    dy = NY // 2 + ((along + 1) // 2) * (1 - 2 * (along % 2))
    return ((y + dy) % NY) * NZ + (z + dz + NZ) % NZ


def routing(ids, weights):
    lane = lax.broadcasted_iota(jnp.int32, (ROWS, SLOTS), 1)
    expert = (lane // BLOCK).astype(F32)
    named = jnp.zeros((ROWS, SLOTS), F32)
    weight = jnp.zeros((ROWS, SLOTS), F32)
    for k in range(TOP):
        hit = ids[:, k : k + 1] == expert
        named = named + jnp.where(hit, 1.0, 0.0)
        weight = weight + jnp.where(hit, weights[:, k : k + 1], 0.0)
    before = (
        lax.broadcasted_iota(jnp.int32, (ROWS, ROWS), 1)
        < lax.broadcasted_iota(jnp.int32, (ROWS, ROWS), 0)
    ).astype(F32)
    earlier = dot(before.astype(BF16), named.astype(BF16))
    placed = jnp.where(earlier == (lane % CAP).astype(F32), named, 0.0)
    first = (lane % BLOCK) < CAP
    from_slots = jnp.concatenate(
        [jnp.where(first, placed, 0.0), jnp.where(first, 0.0, placed)], axis=0
    )
    slot_weight = jnp.sum(placed * weight, axis=0, keepdims=True)
    both = jnp.concatenate(
        [from_slots, jnp.broadcast_to(slot_weight, (128 - 2 * ROWS, SLOTS))], axis=0
    )
    turned = both.T
    to_slots = turned[:, : 2 * ROWS].astype(BF16)
    slot_weights = jnp.broadcast_to(turned[:, 2 * ROWS : 2 * ROWS + 1], (SLOTS, 128))
    return to_slots, from_slots.astype(BF16), slot_weights


def halves(value):
    return jnp.concatenate([value[:, :HALF], value[:, HALF:]], axis=0)


def first_rows(shape):
    return (lax.broadcasted_iota(jnp.int32, shape, 0) % BLOCK) < CAP


def by_half(first, second):
    own = jnp.where(first_rows(first.shape), first, second)
    grouped = own.reshape(EXPERTS, BLOCK, own.shape[-1])
    return (grouped + pltpu.roll(grouped, CAP, 1)).reshape(own.shape)


def scale_rows(rows, slot_weights):
    return rows * jnp.concatenate([slot_weights] * (rows.shape[1] // 128), axis=1)


def kernel(
    inputs_ref,
    ids_ref,
    gates_ref,
    gain_ref,
    top_ref,
    w_gate_hbm,
    w_up_hbm,
    w_down_hbm,
    out_ref,
    grad_gate_ref,
    grad_up_ref,
    grad_down_ref,
    gain_out_ref,
    w_gate,
    w_up,
    w_down,
    meta_own,
    meta_next,
    own_to,
    own_from,
    own_weight,
    next_to,
    next_weight,
    unit,
    scale,
    cot,
    cot_out,
    in_send,
    in_recv,
    top_send,
    cot_send,
    cot_recv,
    ret_send,
    ret_recv,
    coef_gate,
    coef_up,
    act,
    d_gate_rows,
    d_up_rows,
    acc_gate,
    acc_up,
    acc_down,
    gain_part,
    gain_all,
    load_sem,
    meta_send_sem,
    meta_recv_sem,
    in_send_sem,
    in_recv_sem,
    top_send_sem,
    cot_send_sem,
    cot_recv_sem,
    res_send_sem,
    res_recv_sem,
    ret_send_sem,
    ret_recv_sem,
    gain_send_sem,
    gain_recv_sem,
):
    section = lax.axis_index("section")
    index = lax.axis_index("expert")
    is_top = section == SECTIONS - 1
    is_last = section == 0

    loads = [
        pltpu.make_async_copy(source, target, load_sem.at[number])
        for number, (source, target) in enumerate(
            [(w_gate_hbm, w_gate), (w_up_hbm, w_up), (w_down_hbm, w_down)]
        )
    ]
    for load in loads:
        load.start()

    barrier = pltpu.get_barrier_semaphore()

    def greet(to_section, count):
        def step(number, carry):
            pl.semaphore_signal(
                barrier, inc=1, device_id=(to_section, peer(number, index)), device_id_type=MESH
            )
            return carry

        lax.fori_loop(0, count, step, 0)

    greet(section, EXPERTS - 1)

    @pl.when(jnp.logical_not(is_top))
    def _():
        greet(section + 1, EXPERTS)

    @pl.when(jnp.logical_not(is_last))
    def _():
        pl.semaphore_signal(
            barrier, inc=1, device_id=(section - 1, index), device_id_type=MESH
        )

    def send_blocks(source, target, m, to_section, send_sem, recv_sem, count):
        def step(number, carry):
            to = peer(number, index)
            pltpu.make_async_remote_copy(
                source.at[m, to],
                target.at[m, index],
                send_sem.at[m],
                recv_sem.at[m],
                device_id=(to_section, to),
                device_id_type=MESH,
            ).start()
            return carry

        lax.fori_loop(0, count, step, 0)

    def keep_own(source, target, m, recv_sem):
        pltpu.make_async_copy(
            source.at[m, index], target.at[m, index], recv_sem.at[m]
        ).start()

    def wait_blocks(ref, m, sem, count):
        part = ref.at[m, pl.ds(0, count)]
        pltpu.make_async_copy(part, part, sem.at[m]).wait()

    def prepare(m):
        values = inputs_ref[0, m].astype(F32)
        scales = lax.rsqrt(jnp.mean(values * values, axis=-1, keepdims=True) + epsilon)
        unit_rows = values * scales
        normed = (unit_rows * gain_ref[...]).astype(BF16)
        unit[m] = halves(unit_rows)
        scale[m] = jnp.broadcast_to(scales, (ROWS, 128))
        ids = ids_ref[0, m].astype(F32)
        weights = gates_ref[0, m]
        to_slots, from_slots, slot_weights = routing(ids, weights)
        own_to[m] = to_slots
        own_from[m] = from_slots
        own_weight[m] = slot_weights
        meta_own[m] = jnp.concatenate(
            [ids, weights, jnp.zeros((ROWS, 128 - 2 * TOP), F32)], axis=1
        )
        in_send[m] = dot(to_slots, halves(normed)).astype(BF16).reshape(EXPERTS, BLOCK, HALF)

        @pl.when(is_top)
        def _():
            rows = halves(top_ref[m])
            cot[m] = rows
            top_send[m] = (
                scale_rows(dot(to_slots, rows), slot_weights)
                .astype(BF16)
                .reshape(EXPERTS, BLOCK, HALF)
            )

    def send_inputs(m):
        send_blocks(in_send, in_recv, m, section, in_send_sem, in_recv_sem, EXPERTS - 1)
        keep_own(in_send, in_recv, m, in_recv_sem)

    def send_top(m):
        send_blocks(top_send, cot_recv, m, section, top_send_sem, cot_recv_sem, EXPERTS - 1)
        keep_own(top_send, cot_recv, m, cot_recv_sem)

    prepare(0)
    pl.semaphore_wait(
        barrier,
        EXPERTS - 1
        + jnp.where(is_last, 0, EXPERTS)
        + jnp.where(is_top, 0, 1),
    )
    send_inputs(0)
    pl.when(is_top)(lambda: send_top(0))

    def prepare_rest(m, carry):
        prepare(m)

        @pl.when(jnp.logical_not(is_top))
        def _():
            send_inputs(m)

        return carry

    lax.fori_loop(1, MICRO, prepare_rest, 0)

    @pl.when(jnp.logical_not(is_top))
    def _():
        pltpu.make_async_remote_copy(
            meta_own,
            meta_next,
            meta_send_sem,
            meta_recv_sem,
            device_id=(section + 1, index),
            device_id_type=MESH,
        ).start()

    acc_gate[...] = jnp.zeros_like(acc_gate)
    acc_up[...] = jnp.zeros_like(acc_up)
    acc_down[...] = jnp.zeros_like(acc_down)
    gain_part[...] = jnp.zeros_like(gain_part)

    @pl.when(jnp.logical_not(is_last))
    def _():
        pltpu.make_async_copy(meta_next, meta_next, meta_recv_sem).wait()

        def step(m, carry):
            known = meta_next[m]
            to_slots, _, slot_weights = routing(known[:, :TOP], known[:, TOP : 2 * TOP])
            next_to[m] = to_slots
            next_weight[m] = slot_weights
            return carry

        lax.fori_loop(0, MICRO, step, 0)

    for load in loads:
        load.wait()

    def before(m):
        wait_blocks(in_recv, m, in_recv_sem, EXPERTS)
        rows = in_recv[m].reshape(SLOTS, HALF)
        pre_gate = by_half(dot(rows, w_gate[:HALF]), dot(rows, w_gate[HALF:]))
        pre_up = by_half(dot(rows, w_up[:HALF]), dot(rows, w_up[HALF:]))
        sigma = jax.nn.sigmoid(pre_gate)
        silu = pre_gate * sigma
        act[m] = (silu * pre_up).astype(BF16)
        coef_gate[m] = pre_up * sigma * (1.0 + pre_gate * (1.0 - sigma))
        coef_up[m] = silu

    before(0)

    def one_micro(m, carry):
        wait_blocks(cot_recv, m, cot_recv_sem, EXPERTS)
        rows = cot_recv[m].reshape(SLOTS, HALF)
        d_act = by_half(
            dot(rows, w_down[:, :HALF], 1, 1), dot(rows, w_down[:, HALF:], 1, 1)
        )
        d_gate = (d_act * coef_gate[m]).astype(BF16)
        d_up = (d_act * coef_up[m]).astype(BF16)
        d_gate_rows[...] = d_gate
        d_up_rows[...] = d_up
        low = dot(d_gate, w_gate[:HALF], 1, 1) + dot(d_up, w_up[:HALF], 1, 1)
        high = dot(d_gate, w_gate[HALF:], 1, 1) + dot(d_up, w_up[HALF:], 1, 1)
        ret_send[m] = (
            jnp.where(first_rows(low.shape), low, high)
            .astype(BF16)
            .reshape(EXPERTS, BLOCK, HALF)
        )
        send_blocks(ret_send, ret_recv, m, section, ret_send_sem, ret_recv_sem, EXPERTS - 1)
        keep_own(ret_send, ret_recv, m, ret_recv_sem)

        if m < MICRO - 1:

            @pl.when(is_top)
            def _():
                send_inputs(m + 1)
                send_top(m + 1)

        in_rows = in_recv[m].reshape(SLOTS, HALF)
        cot_rows = cot_recv[m].reshape(SLOTS, HALF)
        left = (lax.broadcasted_iota(jnp.int32, (HIDDEN, SLOTS), 1) % BLOCK) < CAP
        for rows_ref, total, others in (
            (d_gate_rows[...], acc_gate, in_rows),
            (d_up_rows[...], acc_up, in_rows),
            (act[m], acc_down, cot_rows),
        ):
            turned = rows_ref.astype(F32).T
            total[0] += dot(jnp.where(left, turned, 0.0).astype(BF16), others)
            total[1] += dot(jnp.where(left, 0.0, turned).astype(BF16), others)

        if m < MICRO - 1:
            before(m + 1)
        else:
            for half in range(2):
                span = pl.ds(half * HALF, HALF)
                grad_gate_ref[span, :] = acc_gate[half].T.astype(BF16)
                grad_up_ref[span, :] = acc_up[half].T.astype(BF16)
                grad_down_ref[:, span] = acc_down[half].astype(BF16)

        @pl.when(jnp.logical_not(is_top))
        def _():
            pltpu.make_async_copy(cot.at[m], cot.at[m], res_recv_sem.at[m]).wait()

        wait_blocks(ret_recv, m, ret_recv_sem, EXPERTS)
        d_normed = dot(own_from[m], ret_recv[m].reshape(SLOTS, HALF))
        units = unit[m]
        gained = d_normed * units
        gain_part[...] += jnp.concatenate(
            [
                jnp.sum(gained[:ROWS], axis=0, keepdims=True),
                jnp.sum(gained[ROWS:], axis=0, keepdims=True),
            ],
            axis=0,
        )
        gain = jnp.concatenate(
            [
                jnp.broadcast_to(gain_ref[:, :HALF], (ROWS, HALF)),
                jnp.broadcast_to(gain_ref[:, HALF:], (ROWS, HALF)),
            ],
            axis=0,
        )
        scaled = d_normed * gain
        sums = jnp.sum(scaled * units, axis=-1, keepdims=True)
        mean = (sums[:ROWS] + sums[ROWS:]) * (1.0 / WIDTH)
        means = jnp.concatenate([mean, mean], axis=0)
        scales = scale[m][:, :1]
        scales = jnp.concatenate([scales, scales], axis=0)
        grad = (cot[m].astype(F32) + scales * (scaled - units * means)).astype(BF16)
        out_ref[0, m, :, :HALF] = grad[:ROWS]
        out_ref[0, m, :, HALF:] = grad[ROWS:]

        @pl.when(jnp.logical_not(is_last))
        def _():
            cot_send[m] = (
                scale_rows(dot(next_to[m], grad), next_weight[m])
                .astype(BF16)
                .reshape(EXPERTS, BLOCK, HALF)
            )
            cot_out[m] = grad
            send_blocks(
                cot_send, cot_recv, m, section - 1, cot_send_sem, cot_recv_sem, EXPERTS
            )
            pltpu.make_async_remote_copy(
                cot_out.at[m],
                cot.at[m],
                res_send_sem.at[m],
                res_recv_sem.at[m],
                device_id=(section - 1, index),
                device_id_type=MESH,
            ).start()

        return carry

    for m in range(MICRO):
        one_micro(m, 0)

    gain_all[index] = gain_part[...]

    def send_gain(number, carry):
        pltpu.make_async_remote_copy(
            gain_part,
            gain_all.at[index],
            gain_send_sem,
            gain_recv_sem,
            device_id=(section, peer(number, index)),
            device_id_type=MESH,
        ).start()
        return carry

    lax.fori_loop(0, EXPERTS - 1, send_gain, 0)

    def drain(m, carry):
        wait_blocks(in_send, m, in_send_sem, EXPERTS - 1)
        wait_blocks(ret_send, m, ret_send_sem, EXPERTS - 1)

        @pl.when(is_top)
        def _():
            wait_blocks(top_send, m, top_send_sem, EXPERTS - 1)

        @pl.when(jnp.logical_not(is_last))
        def _():
            wait_blocks(cot_send, m, cot_send_sem, EXPERTS)
            pltpu.make_async_copy(cot_out.at[m], cot_out.at[m], res_send_sem.at[m]).wait()

        return carry

    lax.fori_loop(0, MICRO, drain, 0)

    @pl.when(jnp.logical_not(is_top))
    def _():
        pltpu.make_async_copy(meta_own, meta_own, meta_send_sem).wait()

    others = gain_all.at[pl.ds(0, EXPERTS - 1)]
    pltpu.make_async_copy(others, others, gain_recv_sem).wait()
    pltpu.make_async_copy(others, others, gain_send_sem).wait()
    total = jnp.sum(gain_all[...], axis=0)
    gain_out_ref[:, :HALF] = total[:1]
    gain_out_ref[:, HALF:] = total[1:]


def local(layer_inputs, expert_ids, gate_weights, norm_gain, w_gate, w_up, w_down, top_cotangent):
    blocks = pltpu.VMEM((MICRO, EXPERTS, BLOCK, HALF), BF16)
    vmem = pl.BlockSpec(memory_space=pltpu.VMEM)
    hbm = pl.BlockSpec(memory_space=pl.ANY)
    dma = pltpu.SemaphoreType.DMA
    outs = pl.pallas_call(
        kernel,
        out_shape=(
            jax.ShapeDtypeStruct((1, MICRO, ROWS, WIDTH), BF16),
            jax.ShapeDtypeStruct((WIDTH, HIDDEN), BF16),
            jax.ShapeDtypeStruct((WIDTH, HIDDEN), BF16),
            jax.ShapeDtypeStruct((HIDDEN, WIDTH), BF16),
            jax.ShapeDtypeStruct((1, WIDTH), F32),
        ),
        in_specs=[vmem] * 5 + [hbm] * 3,
        out_specs=(vmem,) * 5,
        scratch_shapes=[
            pltpu.VMEM((WIDTH, HIDDEN), BF16),
            pltpu.VMEM((WIDTH, HIDDEN), BF16),
            pltpu.VMEM((HIDDEN, WIDTH), BF16),
            pltpu.VMEM((MICRO, ROWS, 128), F32),
            pltpu.VMEM((MICRO, ROWS, 128), F32),
            pltpu.VMEM((MICRO, SLOTS, 2 * ROWS), BF16),
            pltpu.VMEM((MICRO, 2 * ROWS, SLOTS), BF16),
            pltpu.VMEM((MICRO, SLOTS, 128), F32),
            pltpu.VMEM((MICRO, SLOTS, 2 * ROWS), BF16),
            pltpu.VMEM((MICRO, SLOTS, 128), F32),
            pltpu.VMEM((MICRO, 2 * ROWS, HALF), F32),
            pltpu.VMEM((MICRO, ROWS, 128), F32),
            pltpu.VMEM((MICRO, 2 * ROWS, HALF), BF16),
            pltpu.VMEM((MICRO, 2 * ROWS, HALF), BF16),
            blocks,
            blocks,
            blocks,
            blocks,
            blocks,
            blocks,
            blocks,
            pltpu.VMEM((MICRO, SLOTS, HIDDEN), F32),
            pltpu.VMEM((MICRO, SLOTS, HIDDEN), F32),
            pltpu.VMEM((MICRO, SLOTS, HIDDEN), BF16),
            pltpu.VMEM((SLOTS, HIDDEN), BF16),
            pltpu.VMEM((SLOTS, HIDDEN), BF16),
            pltpu.VMEM((2, HIDDEN, HALF), F32),
            pltpu.VMEM((2, HIDDEN, HALF), F32),
            pltpu.VMEM((2, HIDDEN, HALF), F32),
            pltpu.VMEM((2, HALF), F32),
            pltpu.VMEM((EXPERTS, 2, HALF), F32),
            dma((3,)),
            dma,
            dma,
            dma((MICRO,)),
            dma((MICRO,)),
            dma((MICRO,)),
            dma((MICRO,)),
            dma((MICRO,)),
            dma((MICRO,)),
            dma((MICRO,)),
            dma((MICRO,)),
            dma((MICRO,)),
            dma,
            dma,
        ],
        compiler_params=pltpu.CompilerParams(
            collective_id=0, has_side_effects=True, vmem_limit_bytes=56 * 1024 * 1024
        ),
    )(
        layer_inputs,
        expert_ids,
        gate_weights,
        norm_gain,
        top_cotangent,
        w_gate[0, 0],
        w_up[0, 0],
        w_down[0, 0],
    )
    return (outs[0], outs[1][None, None], outs[2][None, None], outs[3][None, None], outs[4])


def solution(mesh):
    in_specs = (
        P("section", None, "expert", None),
        P("section", None, "expert", None),
        P("section", None, "expert", None),
        P("section", None),
        P("section", "expert", None, None),
        P("section", "expert", None, None),
        P("section", "expert", None, None),
        P(None, "expert", None),
    )
    out_specs = (
        P("section", None, "expert", None),
        P("section", "expert", None, None),
        P("section", "expert", None, None),
        P("section", "expert", None, None),
        P("section", None),
    )
    return jax.shard_map(local, mesh=mesh, in_specs=in_specs, out_specs=out_specs, check_vma=False)
```

time: 1070 us -> 337 us (0.31)
  the two profiles are of different devices: /device:TPU:4 before, /device:TPU:8 now
where the time goes in v1:
time: 337 us
  Pallas kernels  327 us (97%)
  local copies, waits for them, and re-layouts  8.92 us (3%)
    pallas_call x1, Pallas kernels, local(): pl.pallas_call(kernel, out_shape=(jax.ShapeDtypeStruct((1, MICRO, ROWS, W...  327 us
    unnamed x17, local copies, waits for them, and re-layouts  8.92 us

profile of v1, /device:TPU:8, one launch (start us, length us, event | category | flops | bytes accessed | tf_op | source)
XLA Modules:
  0.0 336.7 jit_solution(18129917958125102542)
XLA Ops:
  0.6 0.0 copy-start.4
  0.6 1.4 copy.13.ids_ref
  2.1 0.0 copy-done.4
  2.1 0.7 copy.14.gates_ref
  2.8 327.1 %shard_map.119 = (bf16[1,4,32,2048]{3,2,1,0:T(8,128)(2,1)}, bf16[2048,256]{1,0:T(8,128)(2,1)}, bf16[2048,256]{1,0:T(8,128)(2,1)}, bf16[256,2048]{1,0:T(8,128)(2,1)}, f32[1,2048]{1,0:T(1,128)}) custom-call(bf16[1,4,32,2048]{3,2,1,0:T(8,128)(2,1)} %inputs_ref.1, s32[1,4,32,3]{3,2,1,0:T(8,128)} %copy.13.ids_ref, f32[1,4,32,3]{3,2,1,0:T(8,128)} %copy.14.gates_ref, ...), custom_call_target="tpu_custom_call" | custom-call | tf_op jit(solution)/shard_map/pallas_call | solution.py:467
  329.9 0.0 copy-start.2
  329.9 2.0 copy.20
  331.9 0.0 copy-done.2
  331.9 0.0 copy-start.1
  331.9 1.0 copy.21
  332.9 0.6 copy-done.1
  333.5 0.0 copy-start
  333.5 1.0 copy.22
  334.5 0.6 copy-done
  335.1 0.0 copy-start.3
  335.1 1.0 copy.23
  336.1 0.0 copy-done.3
  336.1 0.6 copy.24
Async XLA Ops:
  0.6 1.4 copy-start.4
  329.9 2.0 copy-start.2
  331.9 1.6 copy-start.1
  333.5 1.6 copy-start
  335.1 1.0 copy-start.3

commit v2 on v1

--- a/solution.py
+++ b/solution.py
@@ -24,6 +24,7 @@
 CAP = 4
 BLOCK = 2 * CAP
 SLOTS = EXPERTS * BLOCK
+PART = EXPERTS // 2
 
 
 def dot(left, right, left_dim=1, right_dim=0):
@@ -32,23 +33,33 @@
     )
 
 
-def peer(step, index):
-    y, z = index // NZ, index % NZ
+def offsets(step):
     across, along = step // NY, step % NY
     dz = NZ // 2 + ((across + 1) // 2) * (1 - 2 * (across % 2))
     dy = NY // 2 + ((along + 1) // 2) * (1 - 2 * (along % 2))
-    return ((y + dy) % NY) * NZ + (z + dz + NZ) % NZ
-
-
-def routing(ids, weights):
+    return dy % NY, dz % NZ
+
+
+def peer(step, index):
+    dy, dz = offsets(step)
+    return ((index // NZ + dy) % NY) * NZ + (index % NZ + dz) % NZ
+
+
+def source(step, index):
+    dy, dz = offsets(step)
+    return ((index // NZ - dy + NY) % NY) * NZ + (index % NZ - dz + NZ) % NZ
+
+
+def routing(known, index):
+    columns = known.T[:ROWS]
     lane = lax.broadcasted_iota(jnp.int32, (ROWS, SLOTS), 1)
-    expert = (lane // BLOCK).astype(F32)
+    expert = peer(lane // BLOCK, index).astype(F32)
     named = jnp.zeros((ROWS, SLOTS), F32)
     weight = jnp.zeros((ROWS, SLOTS), F32)
     for k in range(TOP):
-        hit = ids[:, k : k + 1] == expert
+        hit = columns[:, k : k + 1] == expert
         named = named + jnp.where(hit, 1.0, 0.0)
-        weight = weight + jnp.where(hit, weights[:, k : k + 1], 0.0)
+        weight = weight + jnp.where(hit, columns[:, TOP + k : TOP + k + 1], 0.0)
     before = (
         lax.broadcasted_iota(jnp.int32, (ROWS, ROWS), 1)
         < lax.broadcasted_iota(jnp.int32, (ROWS, ROWS), 0)
@@ -79,7 +90,7 @@
 
 def by_half(first, second):
     own = jnp.where(first_rows(first.shape), first, second)
-    grouped = own.reshape(EXPERTS, BLOCK, own.shape[-1])
+    grouped = own.reshape(own.shape[0] // BLOCK, BLOCK, own.shape[-1])
     return (grouped + pltpu.roll(grouped, CAP, 1)).reshape(own.shape)
 
 
@@ -106,6 +117,7 @@
     w_down,
     meta_own,
     meta_next,
+    meta_help,
     own_to,
     own_from,
     own_weight,
@@ -115,6 +127,8 @@
     scale,
     cot,
     cot_out,
+    normed,
+    help_rows,
     in_send,
     in_recv,
     top_send,
@@ -135,6 +149,10 @@
     load_sem,
     meta_send_sem,
     meta_recv_sem,
+    meta_help_send_sem,
+    meta_help_recv_sem,
+    rows_send_sem,
+    rows_recv_sem,
     in_send_sem,
     in_recv_sem,
     top_send_sem,
@@ -172,92 +190,145 @@
 
         lax.fori_loop(0, count, step, 0)
 
+    helps_inputs = section == 1
+    helps_top = section == 0
+    helps_second = section == 3
+    is_helper = helps_inputs | helps_top | helps_second
+    is_second = section == SECTIONS - 2
+
+    def hello(to_section):
+        pl.semaphore_signal(
+            barrier, inc=1, device_id=(to_section, index), device_id_type=MESH
+        )
+
     greet(section, EXPERTS - 1)
-
-    @pl.when(jnp.logical_not(is_top))
-    def _():
-        greet(section + 1, EXPERTS)
-
-    @pl.when(jnp.logical_not(is_last))
-    def _():
-        pl.semaphore_signal(
-            barrier, inc=1, device_id=(section - 1, index), device_id_type=MESH
-        )
-
-    def send_blocks(source, target, m, to_section, send_sem, recv_sem, count):
+    pl.when(jnp.logical_not(is_top))(lambda: greet(section + 1, EXPERTS))
+    pl.when(jnp.logical_not(is_last))(lambda: hello(section - 1))
+    pl.when(helps_inputs | helps_top)(lambda: hello(SECTIONS - 1))
+    pl.when(helps_second)(lambda: hello(SECTIONS - 2))
+
+    def send_blocks(source_ref, target, m, to_section, send_sem, recv_sem, first, last, back=False):
         def step(number, carry):
-            to = peer(number, index)
+            to = source(number, index) if back else peer(number, index)
             pltpu.make_async_remote_copy(
-                source.at[m, to],
-                target.at[m, index],
-                send_sem.at[m],
-                recv_sem.at[m],
+                source_ref.at[m, number],
+                target.at[m, number],
+                send_sem,
+                recv_sem,
                 device_id=(to_section, to),
                 device_id_type=MESH,
             ).start()
             return carry
 
-        lax.fori_loop(0, count, step, 0)
-
-    def keep_own(source, target, m, recv_sem):
+        lax.fori_loop(first, last, step, 0)
+
+    def keep_own(source_ref, target, m, recv_sem):
         pltpu.make_async_copy(
-            source.at[m, index], target.at[m, index], recv_sem.at[m]
+            source_ref.at[m, EXPERTS - 1], target.at[m, EXPERTS - 1], recv_sem
         ).start()
 
-    def wait_blocks(ref, m, sem, count):
-        part = ref.at[m, pl.ds(0, count)]
-        pltpu.make_async_copy(part, part, sem.at[m]).wait()
+    def wait_blocks(ref, m, sem, first, count):
+        part = ref.at[m, pl.ds(first, count)]
+        pltpu.make_async_copy(part, part, sem).wait()
+
+    def send_one(source_ref, target, to_section, send_sem, recv_sem):
+        pltpu.make_async_remote_copy(
+            source_ref,
+            target,
+            send_sem,
+            recv_sem,
+            device_id=(to_section, index),
+            device_id_type=MESH,
+        ).start()
+
+    meta_own[...] = jnp.zeros_like(meta_own)
+    for m in range(MICRO):
+        for k in range(TOP):
+            meta_own[m, k : k + 1, 0:ROWS] = ids_ref[0, k, m : m + 1].astype(F32)
+            meta_own[m, TOP + k : TOP + k + 1, 0:ROWS] = gates_ref[0, k, m : m + 1]
 
     def prepare(m):
         values = inputs_ref[0, m].astype(F32)
         scales = lax.rsqrt(jnp.mean(values * values, axis=-1, keepdims=True) + epsilon)
         unit_rows = values * scales
-        normed = (unit_rows * gain_ref[...]).astype(BF16)
+        normed[m] = halves((unit_rows * gain_ref[...]).astype(BF16))
         unit[m] = halves(unit_rows)
         scale[m] = jnp.broadcast_to(scales, (ROWS, 128))
-        ids = ids_ref[0, m].astype(F32)
-        weights = gates_ref[0, m]
-        to_slots, from_slots, slot_weights = routing(ids, weights)
+        to_slots, from_slots, slot_weights = routing(meta_own[m], index)
         own_to[m] = to_slots
         own_from[m] = from_slots
         own_weight[m] = slot_weights
-        meta_own[m] = jnp.concatenate(
-            [ids, weights, jnp.zeros((ROWS, 128 - 2 * TOP), F32)], axis=1
+        pl.when(is_top)(lambda: cot.__setitem__(m, halves(top_ref[m])))
+
+    def spread(placing, rows):
+        return dot(placing, rows).astype(BF16).reshape(EXPERTS, BLOCK, HALF)
+
+    def spread_scaled(placing, rows, weights):
+        scaled = scale_rows(dot(placing, rows), weights)
+        return scaled.astype(BF16).reshape(placing.shape[0] // BLOCK, BLOCK, HALF)
+
+    def send_inputs(m):
+        in_send[m] = spread(own_to[m], normed[m])
+        send_blocks(
+            in_send, in_recv, m, section, in_send_sem.at[m], in_recv_sem.at[m], 0, EXPERTS - 1
         )
-        in_send[m] = dot(to_slots, halves(normed)).astype(BF16).reshape(EXPERTS, BLOCK, HALF)
-
-        @pl.when(is_top)
-        def _():
-            rows = halves(top_ref[m])
-            cot[m] = rows
-            top_send[m] = (
-                scale_rows(dot(to_slots, rows), slot_weights)
-                .astype(BF16)
-                .reshape(EXPERTS, BLOCK, HALF)
-            )
-
-    def send_inputs(m):
-        send_blocks(in_send, in_recv, m, section, in_send_sem, in_recv_sem, EXPERTS - 1)
-        keep_own(in_send, in_recv, m, in_recv_sem)
-
-    def send_top(m):
-        send_blocks(top_send, cot_recv, m, section, top_send_sem, cot_recv_sem, EXPERTS - 1)
-        keep_own(top_send, cot_recv, m, cot_recv_sem)
+        keep_own(in_send, in_recv, m, in_recv_sem.at[m])
 
     prepare(0)
     pl.semaphore_wait(
         barrier,
         EXPERTS - 1
         + jnp.where(is_last, 0, EXPERTS)
-        + jnp.where(is_top, 0, 1),
+        + jnp.where(is_top, 2, 1)
+        + jnp.where(is_helper, EXPERTS, 0)
+        + jnp.where(is_second, 1, 0),
     )
-    send_inputs(0)
-    pl.when(is_top)(lambda: send_top(0))
+
+    @pl.when(is_top)
+    def _():
+        send_inputs(0)
+        top_send[0] = spread_scaled(own_to[0], cot[0], own_weight[0])
+        for part in range(2):
+            send_blocks(
+                top_send,
+                cot_recv,
+                0,
+                section,
+                top_send_sem.at[0],
+                cot_recv_sem.at[0, part],
+                part * PART,
+                PART + part * (PART - 1),
+            )
+        keep_own(top_send, cot_recv, 0, cot_recv_sem.at[0, 1])
+        greet(1, EXPERTS)
+        greet(0, EXPERTS)
+        send_one(meta_own, meta_help, 1, meta_help_send_sem.at[0], meta_help_recv_sem)
+        send_one(meta_own, meta_help, 0, meta_help_send_sem.at[1], meta_help_recv_sem)
+
+    @pl.when(is_second)
+    def _():
+        greet(3, EXPERTS)
+        send_one(meta_own, meta_help, 3, meta_help_send_sem.at[0], meta_help_recv_sem)
+        send_one(normed.at[0], help_rows.at[0], 3, rows_send_sem.at[0], rows_recv_sem.at[0])
+
+    pl.when(section < SECTIONS - 2)(lambda: send_inputs(0))
+
+    @pl.when(jnp.logical_not(is_top))
+    def _():
+        send_one(meta_own, meta_next, section + 1, meta_send_sem, meta_recv_sem)
 
     def prepare_rest(m, carry):
         prepare(m)
 
-        @pl.when(jnp.logical_not(is_top))
+        @pl.when(is_top)
+        def _():
+            send_one(normed.at[m], help_rows.at[m], 1, rows_send_sem.at[m], rows_recv_sem.at[m])
+
+        @pl.when(is_second)
+        def _():
+            send_one(normed.at[m], help_rows.at[m], 3, rows_send_sem.at[m], rows_recv_sem.at[m])
+
+        @pl.when((section < SECTIONS - 2) & jnp.logical_not(is_helper))
         def _():
             send_inputs(m)
 
@@ -265,16 +336,52 @@
 
     lax.fori_loop(1, MICRO, prepare_rest, 0)
 
-    @pl.when(jnp.logical_not(is_top))
+    @pl.when(is_helper)
     def _():
-        pltpu.make_async_remote_copy(
-            meta_own,
-            meta_next,
-            meta_send_sem,
-            meta_recv_sem,
-            device_id=(section + 1, index),
-            device_id_type=MESH,
-        ).start()
+        pltpu.make_async_copy(meta_help, meta_help, meta_help_recv_sem).wait()
+
+        def help_one(m, carry):
+            placing, _, weights = routing(meta_help[m], index)
+
+            @pl.when(helps_top)
+            def _():
+                top_send[m] = spread_scaled(placing, halves(top_ref[m]), weights)
+                for part in range(2):
+                    send_blocks(
+                        top_send,
+                        cot_recv,
+                        m,
+                        SECTIONS - 1,
+                        top_send_sem.at[m],
+                        cot_recv_sem.at[m, part],
+                        part * PART,
+                        PART + part * PART,
+                    )
+
+            @pl.when(jnp.logical_not(helps_top))
+            def _():
+                pltpu.make_async_copy(help_rows.at[m], help_rows.at[m], rows_recv_sem.at[m]).wait()
+                top_send[m] = spread(placing, help_rows[m])
+                send_blocks(
+                    top_send,
+                    in_recv,
+                    m,
+                    jnp.where(helps_second, SECTIONS - 2, SECTIONS - 1),
+                    top_send_sem.at[m],
+                    in_recv_sem.at[m],
+                    0,
+                    EXPERTS,
+                )
+
+            return carry
+
+        lax.fori_loop(jnp.where(helps_second, 0, 1), MICRO, help_one, 0)
+
+        def own_rest(m, carry):
+            send_inputs(m)
+            return carry
+
+        lax.fori_loop(1, MICRO, own_rest, 0)
 
     acc_gate[...] = jnp.zeros_like(acc_gate)
     acc_up[...] = jnp.zeros_like(acc_up)
@@ -286,8 +393,7 @@
         pltpu.make_async_copy(meta_next, meta_next, meta_recv_sem).wait()
 
         def step(m, carry):
-            known = meta_next[m]
-            to_slots, _, slot_weights = routing(known[:, :TOP], known[:, TOP : 2 * TOP])
+            to_slots, _, slot_weights = routing(meta_next[m], index)
             next_to[m] = to_slots
             next_weight[m] = slot_weights
             return carry
@@ -298,7 +404,7 @@
         load.wait()
 
     def before(m):
-        wait_blocks(in_recv, m, in_recv_sem, EXPERTS)
+        wait_blocks(in_recv, m, in_recv_sem.at[m], 0, EXPERTS)
         rows = in_recv[m].reshape(SLOTS, HALF)
         pre_gate = by_half(dot(rows, w_gate[:HALF]), dot(rows, w_gate[HALF:]))
         pre_up = by_half(dot(rows, w_up[:HALF]), dot(rows, w_up[HALF:]))
@@ -311,31 +417,37 @@
     before(0)
 
     def one_micro(m, carry):
-        wait_blocks(cot_recv, m, cot_recv_sem, EXPERTS)
-        rows = cot_recv[m].reshape(SLOTS, HALF)
-        d_act = by_half(
-            dot(rows, w_down[:, :HALF], 1, 1), dot(rows, w_down[:, HALF:], 1, 1)
-        )
-        d_gate = (d_act * coef_gate[m]).astype(BF16)
-        d_up = (d_act * coef_up[m]).astype(BF16)
-        d_gate_rows[...] = d_gate
-        d_up_rows[...] = d_up
-        low = dot(d_gate, w_gate[:HALF], 1, 1) + dot(d_up, w_up[:HALF], 1, 1)
-        high = dot(d_gate, w_gate[HALF:], 1, 1) + dot(d_up, w_up[HALF:], 1, 1)
-        ret_send[m] = (
-            jnp.where(first_rows(low.shape), low, high)
-            .astype(BF16)
-            .reshape(EXPERTS, BLOCK, HALF)
-        )
-        send_blocks(ret_send, ret_recv, m, section, ret_send_sem, ret_recv_sem, EXPERTS - 1)
-        keep_own(ret_send, ret_recv, m, ret_recv_sem)
-
-        if m < MICRO - 1:
-
-            @pl.when(is_top)
-            def _():
-                send_inputs(m + 1)
-                send_top(m + 1)
+        for part in range(2):
+            blocks = pl.ds(part * PART, PART)
+            span = pl.ds(part * PART * BLOCK, PART * BLOCK)
+            wait_blocks(cot_recv, m, cot_recv_sem.at[m, part], part * PART, PART)
+            rows = cot_recv[m, blocks].reshape(PART * BLOCK, HALF)
+            d_act = by_half(
+                dot(rows, w_down[:, :HALF], 1, 1), dot(rows, w_down[:, HALF:], 1, 1)
+            )
+            d_gate = (d_act * coef_gate[m, span]).astype(BF16)
+            d_up = (d_act * coef_up[m, span]).astype(BF16)
+            d_gate_rows[span] = d_gate
+            d_up_rows[span] = d_up
+            low = dot(d_gate, w_gate[:HALF], 1, 1) + dot(d_up, w_up[:HALF], 1, 1)
+            high = dot(d_gate, w_gate[HALF:], 1, 1) + dot(d_up, w_up[HALF:], 1, 1)
+            ret_send[m, blocks] = (
+                jnp.where(first_rows(low.shape), low, high)
+                .astype(BF16)
+                .reshape(PART, BLOCK, HALF)
+            )
+            send_blocks(
+                ret_send,
+                ret_recv,
+                m,
+                section,
+                ret_send_sem.at[m],
+                ret_recv_sem.at[m],
+                part * PART,
+                PART + part * (PART - 1),
+                back=True,
+            )
+        keep_own(ret_send, ret_recv, m, ret_recv_sem.at[m])
 
         in_rows = in_recv[m].reshape(SLOTS, HALF)
         cot_rows = cot_recv[m].reshape(SLOTS, HALF)
@@ -349,9 +461,7 @@
             total[0] += dot(jnp.where(left, turned, 0.0).astype(BF16), others)
             total[1] += dot(jnp.where(left, 0.0, turned).astype(BF16), others)
 
-        if m < MICRO - 1:
-            before(m + 1)
-        else:
+        if m == MICRO - 1:
             for half in range(2):
                 span = pl.ds(half * HALF, HALF)
                 grad_gate_ref[span, :] = acc_gate[half].T.astype(BF16)
@@ -362,7 +472,7 @@
         def _():
             pltpu.make_async_copy(cot.at[m], cot.at[m], res_recv_sem.at[m]).wait()
 
-        wait_blocks(ret_recv, m, ret_recv_sem, EXPERTS)
+        wait_blocks(ret_recv, m, ret_recv_sem.at[m], 0, EXPERTS)
         d_normed = dot(own_from[m], ret_recv[m].reshape(SLOTS, HALF))
         units = unit[m]
         gained = d_normed * units
@@ -392,23 +502,26 @@
 
         @pl.when(jnp.logical_not(is_last))
         def _():
-            cot_send[m] = (
-                scale_rows(dot(next_to[m], grad), next_weight[m])
-                .astype(BF16)
-                .reshape(EXPERTS, BLOCK, HALF)
-            )
+            for part in range(2):
+                span = pl.ds(part * PART * BLOCK, PART * BLOCK)
+                cot_send[m, pl.ds(part * PART, PART)] = spread_scaled(
+                    next_to[m, span], grad, next_weight[m, span]
+                )
+                send_blocks(
+                    cot_send,
+                    cot_recv,
+                    m,
+                    section - 1,
+                    cot_send_sem.at[m],
+                    cot_recv_sem.at[m, part],
+                    part * PART,
+                    PART + part * PART,
+                )
             cot_out[m] = grad
-            send_blocks(
-                cot_send, cot_recv, m, section - 1, cot_send_sem, cot_recv_sem, EXPERTS
-            )
-            pltpu.make_async_remote_copy(
-                cot_out.at[m],
-                cot.at[m],
-                res_send_sem.at[m],
-                res_recv_sem.at[m],
-                device_id=(section - 1, index),
-                device_id_type=MESH,
-            ).start()
+            send_one(cot_out.at[m], cot.at[m], section - 1, res_send_sem.at[m], res_recv_sem.at[m])
+
+        if m < MICRO - 1:
+            before(m + 1)
 
         return carry
 
@@ -431,25 +544,39 @@
     lax.fori_loop(0, EXPERTS - 1, send_gain, 0)
 
     def drain(m, carry):
-        wait_blocks(in_send, m, in_send_sem, EXPERTS - 1)
-        wait_blocks(ret_send, m, ret_send_sem, EXPERTS - 1)
-
-        @pl.when(is_top)
-        def _():
-            wait_blocks(top_send, m, top_send_sem, EXPERTS - 1)
+        wait_blocks(ret_send, m, ret_send_sem.at[m], 0, EXPERTS - 1)
+
+        @pl.when((section < SECTIONS - 2) | (is_top & (m == 0)))
+        def _():
+            wait_blocks(in_send, m, in_send_sem.at[m], 0, EXPERTS - 1)
+
+        @pl.when(is_top & (m == 0))
+        def _():
+            wait_blocks(top_send, m, top_send_sem.at[m], 0, EXPERTS - 1)
+
+        @pl.when(is_helper & ((m > 0) | helps_second))
+        def _():
+            wait_blocks(top_send, m, top_send_sem.at[m], 0, EXPERTS)
+
+        @pl.when(is_second | (is_top & (m > 0)))
+        def _():
+            pltpu.make_async_copy(normed.at[m], normed.at[m], rows_send_sem.at[m]).wait()
 
         @pl.when(jnp.logical_not(is_last))
         def _():
-            wait_blocks(cot_send, m, cot_send_sem, EXPERTS)
+            wait_blocks(cot_send, m, cot_send_sem.at[m], 0, EXPERTS)
             pltpu.make_async_copy(cot_out.at[m], cot_out.at[m], res_send_sem.at[m]).wait()
 
         return carry
 
     lax.fori_loop(0, MICRO, drain, 0)
 
-    @pl.when(jnp.logical_not(is_top))
-    def _():
-        pltpu.make_async_copy(meta_own, meta_own, meta_send_sem).wait()
+    def meta_sent(sem):
+        pltpu.make_async_copy(meta_own, meta_own, sem).wait()
+
+    pl.when(jnp.logical_not(is_top))(lambda: meta_sent(meta_send_sem))
+    pl.when(is_top | is_second)(lambda: meta_sent(meta_help_send_sem.at[0]))
+    pl.when(is_top)(lambda: meta_sent(meta_help_send_sem.at[1]))
 
     others = gain_all.at[pl.ds(0, EXPERTS - 1)]
     pltpu.make_async_copy(others, others, gain_recv_sem).wait()
@@ -479,8 +606,9 @@
             pltpu.VMEM((WIDTH, HIDDEN), BF16),
             pltpu.VMEM((WIDTH, HIDDEN), BF16),
             pltpu.VMEM((HIDDEN, WIDTH), BF16),
-            pltpu.VMEM((MICRO, ROWS, 128), F32),
-            pltpu.VMEM((MICRO, ROWS, 128), F32),
+            pltpu.VMEM((MICRO, 8, 128), F32),
+            pltpu.VMEM((MICRO, 8, 128), F32),
+            pltpu.VMEM((MICRO, 8, 128), F32),
             pltpu.VMEM((MICRO, SLOTS, 2 * ROWS), BF16),
             pltpu.VMEM((MICRO, 2 * ROWS, SLOTS), BF16),
             pltpu.VMEM((MICRO, SLOTS, 128), F32),
@@ -488,6 +616,8 @@
             pltpu.VMEM((MICRO, SLOTS, 128), F32),
             pltpu.VMEM((MICRO, 2 * ROWS, HALF), F32),
             pltpu.VMEM((MICRO, ROWS, 128), F32),
+            pltpu.VMEM((MICRO, 2 * ROWS, HALF), BF16),
+            pltpu.VMEM((MICRO, 2 * ROWS, HALF), BF16),
             pltpu.VMEM((MICRO, 2 * ROWS, HALF), BF16),
             pltpu.VMEM((MICRO, 2 * ROWS, HALF), BF16),
             blocks,
@@ -510,11 +640,15 @@
             dma((3,)),
             dma,
             dma,
-            dma((MICRO,)),
-            dma((MICRO,)),
-            dma((MICRO,)),
-            dma((MICRO,)),
-            dma((MICRO,)),
+            dma((2,)),
+            dma,
+            dma((MICRO,)),
+            dma((MICRO,)),
+            dma((MICRO,)),
+            dma((MICRO,)),
+            dma((MICRO,)),
+            dma((MICRO,)),
+            dma((MICRO, 2)),
             dma((MICRO,)),
             dma((MICRO,)),
             dma((MICRO,)),
@@ -527,8 +661,8 @@
         ),
     )(
         layer_inputs,
-        expert_ids,
-        gate_weights,
+        jnp.transpose(expert_ids, (0, 3, 1, 2)),
+        jnp.transpose(gate_weights, (0, 3, 1, 2)),
         norm_gain,
         top_cotangent,
         w_gate[0, 0],

time: 337 us -> 316 us (0.938)
  Pallas kernels: 327 us -> 308 us
    pallas_call x1, Pallas kernels: 327 us -> 308 us  [local(): pl.pallas_call(kernel, out_shape=(jax.ShapeDtypeStruct((1, MICRO, ROWS, W...]
    unnamed x17 -> x13, local copies, waits for them, and re-layouts: 8.92 us -> 6.75 us
where the time goes in v2:
time: 316 us; the launch traced here: 315 us
  Pallas kernels  308 us (97%)
  local copies, waits for them, and re-layouts  6.75 us (2%)
    pallas_call x1, Pallas kernels, local(): pl.pallas_call(kernel, out_shape=(jax.ShapeDtypeStruct((1, MICRO, ROWS, W...  308 us
    unnamed x13, local copies, waits for them, and re-layouts  6.75 us

profile of v2, /device:TPU:8, one launch (start us, length us, event | category | flops | bytes accessed | tf_op | source)
XLA Modules:
  0.0 315.4 jit_solution(782112782478340444)
XLA Ops:
  0.6 308.0 %shard_map.119 = (bf16[1,4,32,2048]{3,2,1,0:T(8,128)(2,1)}, bf16[2048,256]{1,0:T(8,128)(2,1)}, bf16[2048,256]{1,0:T(8,128)(2,1)}, bf16[256,2048]{1,0:T(8,128)(2,1)}, f32[1,2048]{1,0:T(1,128)}) custom-call(bf16[1,4,32,2048]{3,2,1,0:T(8,128)(2,1)} %inputs_ref.1, s32[1,3,4,32]{3,2,1,0:T(4,128)} %bitcast.14, f32[1,3,4,32]{3,2,1,0:T(4,128)} %bitcast.15, ...), custom_call_target="tpu_custom_call" | custom-call | tf_op jit(solution)/shard_map/pallas_call | solution.py:594
  308.7 0.0 copy-start.2
  308.7 2.0 copy.18
  310.6 0.0 copy-done.2
  310.6 0.0 copy-start.1
  310.6 1.0 copy.19
  311.6 0.6 copy-done.1
  312.3 0.0 copy-start
  312.3 1.0 copy.20
  313.2 0.6 copy-done
  313.9 0.0 copy-start.3
  313.9 1.0 copy.21
  314.8 0.0 copy-done.3
  314.8 0.6 copy.22
Async XLA Ops:
  308.7 2.0 copy-start.2
  310.6 1.6 copy-start.1
  312.3 1.6 copy-start
  313.9 1.0 copy-start.3
